TPU v7x, 128 devices: a whole 4x4x4 slice. The times are simulated.
128 devices in a mesh: cell: 16 (over z, x), level: 4 (over y), rep: 2 (over core).
Axes of the slice: x: 4, y: 4, z: 4, core: 2. Of those that a mesh axis runs over, the one named last changes fastest.
Arguments:
- resident_pos: float32 [2, 32, 128, 2048], P(None, 'rep', 'level', 'cell'), may hold values from -0.5 to 0.5
- resident_strength: float32 [32, 128, 2048], P('rep', 'level', 'cell'), may hold values from -0.51 to 0.51
- mover_pos: float32 [2, 2, 4, 65536], P(None, 'rep', 'level', 'cell'), may hold values from -0.5 to 0.5
- mover_strength: float32 [2, 4, 65536], P('rep', 'level', 'cell'), may hold values from -0.51 to 0.51
- mover_owner: int32 [2, 4, 65536], P('rep', 'level', 'cell'), may hold values from 0 to 15, as said below
- mover_leaf: int32 [2, 4, 65536], P('rep', 'level', 'cell'), may hold values from 0 to 4095, as said below
- mover_slot: int32 [2, 4, 65536], P('rep', 'level', 'cell'), may hold values from 0 to 15
Outputs:
- velocity: float32 [2, 32, 128, 2048], P(None, 'rep', 'level', 'cell')
Inputs may be any that keep to these rules, and one draw needn't show every extreme that they name: `mover_owner`: for one rep and level index, the 4096 movers of one device name one owner at most 1024 times, and one owner is named exactly 1024 times by every device. `mover_leaf`: leaf key y * 128 + x inside the owner's domain; for one rep and level index no (owner, leaf, slot) triple appears twice.
All inputs are finite; a program needn't handle non-finite values.
Results may differ from a plain program's by a relative error of at most 0.0003.
Values sent between devices are 32-bit elements; how exact they have to be, the bound alone decides.
No kernel may reach another device: no remote copies, remote signals or barrier semaphores. Data moves between devices by JAX's collectives and lax.ppermute only.
A program may use at most 192 MiB of HBM per device.

v0:
```python
import math
import jax
import jax.numpy as jnp
import numpy as np
from jax import lax
from jax.sharding import PartitionSpec as P

ORDER = 10
HALO_LEVELS = 4
CAP = 1024
precise = lax.Precision.HIGHEST
blob_square = 0.09


def with_halo(shard, sides, width):
    for axis, dim in sides:
        devices, length = (lax.axis_size(axis), shard.shape[dim])
        up = [(i, (i + 1) % devices) for i in range(devices - 1)]
        down = [(j, i) for i, j in up]
        last = lax.slice_in_dim(shard, length - width, length, axis=dim)
        first = lax.slice_in_dim(shard, 0, width, axis=dim)
        before = lax.ppermute(last, axis, up)
        after = lax.ppermute(first, axis, down)
        shard = jnp.concatenate([before, shard, after], axis=dim)
    return shard


def real_form(matrix):
    top_rows = np.concatenate([matrix.real, -matrix.imag], axis=1)
    low_rows = np.concatenate([matrix.imag, matrix.real], axis=1)
    return np.concatenate([top_rows, low_rows], axis=0)


def child_offset(parity_x, parity_y):
    return complex((parity_x - 0.5) / 2.0, (parity_y - 0.5) / 2.0)


def upward_table(parity_x, parity_y):
    offset = child_offset(parity_x, parity_y)
    matrix = np.zeros((ORDER, ORDER), complex)
    for k in range(ORDER):
        for m in range(k + 1):
            matrix[k, m] = math.comb(k, m) * 0.5**m * offset ** (k - m)
    return real_form(matrix)


def downward_table(parity_x, parity_y):
    offset = child_offset(parity_x, parity_y)
    matrix = np.zeros((ORDER, ORDER), complex)
    for m in range(ORDER):
        for l in range(m, ORDER):
            matrix[m, l] = 0.5 ** (m + 1) * math.comb(l, m) * offset ** (l - m)
    return real_form(matrix)


def far_table(step_x, step_y):
    distance = complex(step_x, step_y)
    matrix = np.zeros((ORDER, ORDER), complex)
    for l in range(ORDER):
        for k in range(ORDER):
            matrix[l, k] = (-1) ** (k + 1) * math.comb(k + l, l) * distance ** (-(k + l + 1))
    return real_form(matrix)


def apply_matrix(matrix, level_field):
    return jnp.einsum(
        "ij,jyx->iyx", jnp.asarray(matrix, dtype=jnp.float32), level_field, precision=precise
    )


def upward(level_field):
    summed = None
    for parity_y in (0, 1):
        for parity_x in (0, 1):
            product = apply_matrix(
                upward_table(parity_x, parity_y), level_field[:, parity_y::2, parity_x::2]
            )
            summed = product if summed is None else summed + product
    return summed


def downward(parent):
    channels, cells_y, cells_x = parent.shape
    pieces = jnp.stack(
        [
            jnp.stack(
                [apply_matrix(downward_table(parity_x, parity_y), parent) for parity_x in (0, 1)]
            )
            for parity_y in (0, 1)
        ]
    )
    return pieces.transpose(2, 3, 0, 4, 1).reshape(channels, 2 * cells_y, 2 * cells_x)


def grouped_far(padded, margin_cells, cells_y, cells_x):
    classes = []
    for parity_y in (0, 1):
        row_parts = []
        for parity_x in (0, 1):
            pieces = []
            blocks = []
            for step_y in range(-2 - parity_y, 4 - parity_y):
                for step_x in range(-2 - parity_x, 4 - parity_x):
                    if max(abs(step_x), abs(step_y)) <= 1:
                        continue
                    first_y = margin_cells + parity_y + step_y
                    first_x = margin_cells + parity_x + step_x
                    pieces.append(
                        padded[:, first_y : first_y + cells_y : 2, first_x : first_x + cells_x : 2]
                    )
                    blocks.append(far_table(step_x, step_y))
            row_parts.append(
                apply_matrix(np.concatenate(blocks, axis=1), jnp.concatenate(pieces, axis=0))
            )
        classes.append(jnp.stack(row_parts))
    joined = jnp.stack(classes)
    return joined.transpose(2, 3, 0, 4, 1).reshape(joined.shape[2], cells_y, cells_x)


def top_far(level_field):
    channels, cells_y, cells_x = level_field.shape
    reach_y = cells_y - 1
    reach_x = cells_x - 1
    padded = jnp.pad(level_field, ((0, 0), (reach_y, reach_y), (reach_x, reach_x)))
    summed = jnp.zeros(level_field.shape, jnp.float32)
    for step_y in range(-reach_y, reach_y + 1):
        for step_x in range(-reach_x, reach_x + 1):
            if max(abs(step_x), abs(step_y)) <= 1:
                continue
            source = padded[
                :,
                reach_y + step_y : reach_y + step_y + cells_y,
                reach_x + step_x : reach_x + step_x + cells_x,
            ]
            summed = summed + apply_matrix(far_table(step_x, step_y), source)
    return summed


def moments(pos_x, pos_y, strength):
    real_power = jnp.ones_like(pos_x)
    imag_power = jnp.zeros_like(pos_x)
    real_rows = []
    imag_rows = []
    for k in range(ORDER):
        real_rows.append(jnp.sum(strength * real_power, axis=0))
        imag_rows.append(jnp.sum(strength * imag_power, axis=0))
        real_power, imag_power = (
            real_power * pos_x - imag_power * pos_y,
            real_power * pos_y + imag_power * pos_x,
        )
    return jnp.stack(real_rows + imag_rows)


def evaluate(local_field, pos_x, pos_y):
    real_acc = jnp.broadcast_to(local_field[ORDER - 1], pos_x.shape)
    imag_acc = jnp.broadcast_to(local_field[2 * ORDER - 1], pos_x.shape)
    for l in range(ORDER - 2, -1, -1):
        real_acc, imag_acc = (
            real_acc * pos_x - imag_acc * pos_y + local_field[l],
            real_acc * pos_y + imag_acc * pos_x + local_field[ORDER + l],
        )
    return (real_acc, imag_acc)


def framing(level_field):
    return with_halo(level_field, (("cell", 2), ("level", 1)), 3)


def local(
    resident_pos, resident_strength, mover_pos, mover_strength, mover_owner, mover_leaf, mover_slot
):
    cell_count = lax.axis_size("cell")
    level_count = lax.axis_size("level")
    half_slots, cells_y, cells_x = resident_strength.shape
    leaves = cells_y * cells_x
    owner_cell = mover_owner.reshape(-1)
    address = mover_slot.reshape(-1) * leaves + mover_leaf.reshape(-1)
    peer_ids = jnp.arange(cell_count, dtype=jnp.int32)
    onehot = (owner_cell[:, None] == peer_ids[None, :]).astype(jnp.int32)
    rank_in_owner = jnp.sum(jnp.cumsum(onehot, axis=0) * onehot, axis=1) - 1
    values = jnp.concatenate([mover_pos.reshape(2, -1), mover_strength.reshape(1, -1)])
    outgoing = (
        jnp.zeros((3, cell_count, CAP), jnp.float32).at[:, owner_cell, rank_in_owner].set(values)
    )
    addresses = (
        jnp.full((1, cell_count, CAP), half_slots * leaves, jnp.int32)
        .at[0, owner_cell, rank_in_owner]
        .set(address)
    )
    arrived, arrived_at = (
        lax.all_to_all(outgoing, "cell", split_axis=1, concat_axis=1, tiled=True),
        lax.all_to_all(addresses, "cell", split_axis=1, concat_axis=1, tiled=True),
    )
    resident = jnp.concatenate([resident_pos.reshape(2, -1), resident_strength.reshape(1, -1)])
    settled = resident.at[:, arrived_at.reshape(-1)].set(arrived.reshape(3, -1), mode="drop")
    particles = settled.reshape(3, half_slots, cells_y, cells_x)
    whole = lax.all_gather(particles, "rep", axis=1, tiled=True)
    framed = with_halo(whole, (("cell", 3), ("level", 2)), 1)
    whole_inner = framed[:, :, 1:-1, 1:-1]
    level_zero = moments(whole_inner[0], whole_inner[1], whole_inner[2])
    owned = [level_zero]
    for k in range(HALO_LEVELS):
        owned.append(upward(owned[-1]))
    framed_levels = [framing(owned[k]) for k in range(HALO_LEVELS)]
    coarse_own = owned[HALO_LEVELS]
    channels, coarse_y, coarse_x = coarse_own.shape
    collected = lax.all_gather(coarse_own[None], ("cell", "level"), axis=0, tiled=True)
    coarse_grid = collected.reshape(cell_count, level_count, channels, coarse_y, coarse_x)
    coarse_grid = coarse_grid.transpose(2, 1, 3, 0, 4).reshape(
        channels, level_count * coarse_y, cell_count * coarse_x
    )
    coarse_fields = [coarse_grid]
    top_level = min(cell_count * cells_x, level_count * cells_y).bit_length() - 1
    for k in range(HALO_LEVELS + 1, top_level + 1):
        coarse_fields.append(upward(coarse_fields[-1]))
    local_field = top_far(coarse_fields[-1])
    for index in range(len(coarse_fields) - 2, -1, -1):
        level_field = coarse_fields[index]
        padded = jnp.pad(level_field, ((0, 0), (3, 3), (3, 3)))
        local_field = grouped_far(padded, 3, level_field.shape[1], level_field.shape[2]) + downward(
            local_field
        )
    local_field = lax.dynamic_slice(
        local_field,
        (0, lax.axis_index("level") * coarse_y, lax.axis_index("cell") * coarse_x),
        (channels, coarse_y, coarse_x),
    )
    for k in range(HALO_LEVELS - 1, -1, -1):
        level_field = owned[k]
        local_field = grouped_far(
            framed_levels[k], 3, level_field.shape[1], level_field.shape[2]
        ) + downward(local_field)
    far_real, far_imag = evaluate(local_field, particles[0], particles[1])
    slot_count = framed.shape[1]
    slot_base = lax.axis_index("rep") * half_slots
    target_slots = slot_base + jnp.arange(half_slots, dtype=jnp.int32)
    keep_mask = (target_slots[:, None] != jnp.arange(slot_count, dtype=jnp.int32)[None, :]).astype(
        jnp.float32
    )[:, :, None, None]
    band_rows = 8

    def near_band(row_start):
        target = lax.dynamic_slice_in_dim(particles, row_start, band_rows, 2)
        real_sum = jnp.zeros((half_slots, band_rows, cells_x), jnp.float32)
        imag_sum = jnp.zeros((half_slots, band_rows, cells_x), jnp.float32)
        for step_y in (-1, 0, 1):
            row_band = lax.dynamic_slice_in_dim(framed, row_start + 1 + step_y, band_rows, 2)
            for step_x in (-1, 0, 1):
                source = row_band[:, :, :, 1 + step_x : 1 + step_x + cells_x]
                gap_x = target[0][:, None] - source[0][None] - step_x
                gap_y = target[1][:, None] - source[1][None] - step_y
                weight = source[2][None] / (gap_x * gap_x + gap_y * gap_y + blob_square)
                if step_x == 0 and step_y == 0:
                    weight = weight * keep_mask
                real_sum = real_sum + jnp.sum(weight * gap_x, axis=1)
                imag_sum = imag_sum - jnp.sum(weight * gap_y, axis=1)
        return jnp.stack([real_sum, imag_sum])

    starts = jnp.arange(0, cells_y, band_rows, dtype=jnp.int32)
    bands = lax.map(near_band, starts)
    near = bands.transpose(1, 2, 0, 3, 4).reshape(2, half_slots, cells_y, cells_x)
    real_part = near[0] + far_real
    imag_part = near[1] + far_imag
    return jnp.stack([imag_part, real_part]) / (2.0 * math.pi)


def solution(mesh):
    return jax.shard_map(
        local,
        mesh=mesh,
        in_specs=(
            P(None, "rep", "level", "cell"),
            P("rep", "level", "cell"),
            P(None, "rep", "level", "cell"),
            P("rep", "level", "cell"),
            P("rep", "level", "cell"),
            P("rep", "level", "cell"),
            P("rep", "level", "cell"),
        ),
        out_specs=P(None, "rep", "level", "cell"),
        check_vma=False,
    )
```

profile of v0, /device:TPU:10, one launch (start us, length us, event | category | flops | bytes accessed | tf_op | source)
XLA Modules:
  0.0 1255.9 jit_solution(15650942823292022477)
XLA Ops:
  7.4 4.6 reduce-window.6
  14.8 16.1 %scatter_custom_fusion.1 = s32[16384]{0:T(1024)} fusion(s32[4096]{0:T(1024)S(1)} %broadcast_select_fusion.1, s32[4096]{0:T(1024)S(1)} %bitcast.975, s32[]{:T(128)} %constant.220.clone.1), kind=kCustom, calls=%fused_computation.410 | custom fusion | bytes 65540
  31.0 8.3 all-to-all-start
  42.2 14.7 %scatter_custom_fusion.2 = f32[3,16384]{0,1:T(8,128)} fusion(s32[4096]{0:T(1024)S(1)} %broadcast_select_fusion, f32[4096,3]{1,0:T(8,128)} %copy.2074, f32[]{:T(128)} %constant.218.clone.1), kind=kCustom, calls=%fused_computation.103 | custom fusion | bytes 197120
  56.9 5.9 copy.2075
  63.7 16.0 %copy.2076 = f32[3,65536]{0,1:T(8,128)} copy(f32[3,65536]{1,0:T(4,128)S(1)} %pad_maximum_fusion.1) | data formatting | bytes 1572864 | tf_op jit(solution)/shard_map/concatenate | solution.py:194
  80.2 7.2 all-to-all-start.1
  87.6 7.2 all-to-all-done.1
  94.8 5.0 copy.2077
  99.8 62.4 %scatter_fusion = f32[3,65536]{0,1:T(8,128)} fusion(f32[3,65536]{0,1:T(8,128)} %copy.2076, s32[16384]{0:T(1024)S(1)} %bitcast.957, f32[16384,3]{1,0:T(8,128)} %copy.2077), kind=kCustom, calls=%fused_computation | custom fusion | bytes 655360 | tf_op jit(solution)/shard_map/scatter | solution.py:195
  162.2 20.2 %copy.2589 = f32[3,16,32,128]{3,2,1,0:T(8,128)} copy(f32[3,16,32,128]{0,3,2,1:T(8,128)} %bitcast.912) | data formatting | bytes 1572864 | tf_op jit(solution)/shard_map/reshape | solution.py:196
  182.5 35.0 %slice_reduce_fusion.1 = (f32[65536]{0:T(1024)}, f32[65536]{0:T(1024)}) fusion(f32[3,65536]{0,1:T(8,128)} %scatter_fusion), kind=kLoop, calls=%fused_computation.102 | loop fusion | bytes 1048576 | tf_op jit(solution)/shard_map/slice | solution.py:233
  247.6 177.4 %all-gather = f32[1280,2,8]{2,1,0:T(2,128)} all-gather(f32[20,2,8]{2,1,0:T(2,128)S(1)} %copy.2384), channel_id=2, replica_groups=mesh['cell'=16,'level'=4,'rep'=2] {'cell','level'}, dimensions={0}, use_global_device_ids=true | all-gather | bytes 83200 | tf_op jit(solution)/shard_map/all_gather | solution.py:207
  569.5 12.1 collective-permute-start.17
  583.5 3.9 collective-permute-start.13
  598.1 3.9 collective-permute-start.9
  606.0 3.9 collective-permute-start.5
  625.3 6.7 collective-permute-start.19
  648.2 4.5 collective-permute-start.1
  667.5 4.5 collective-permute-start.15
  676.8 3.9 slice.1880
  694.7 4.5 collective-permute-start.11
  744.2 4.7 collective-permute-start.7
  758.0 4.5 collective-permute-start.3
  912.6 3.9 slice.1874
  983.4 3.9 slice.1897
  1042.2 9.6 concatenate.134
  1051.8 9.6 concatenate.135
  1061.4 9.6 concatenate.136
  1071.0 9.7 concatenate.137
  1080.7 5.7 convolution_bitcast_fusion.7
  1086.5 3.8 convolution_bitcast_fusion.6
  1090.3 3.8 convolution_bitcast_fusion.5
  1094.1 3.8 convolution_bitcast_fusion.4
  1135.1 5.0 pad_maximum_fusion
  1140.1 103.7 %while.16 = (s32[]{:T(128)}, f32[4,2,16,8,128]{4,3,2,1,0:T(8,128)}, s32[4]{0:T(128)}, f32[3,32,34,130]{3,2,1,0:T(8,128)}, f32[3,16,32,128]{3,2,1,0:T(8,128)}, /*...) while((s32[]{:T(128)}, f32[4,2,16,8,128]{4,3,2,1,0:T(8,128)}, ...), condition=%wide.region_25.26_spmd.clone, body=%wide.region_6.25_spmd.clone.sunk | while | flops 58737680 | bytes 14422976 | solution.py:260
  1145.8 7.4 dynamic-slice_bitcast_fusion.31
  1155.5 4.0 multiply_reduce_fusion.15
  1160.3 5.1 fusion.384
  1171.9 7.1 dynamic-slice_bitcast_fusion.31
  1181.3 4.0 multiply_reduce_fusion.15
  1186.1 5.1 fusion.384
  1197.7 7.3 dynamic-slice_bitcast_fusion.31
  1207.3 4.0 multiply_reduce_fusion.15
  1212.1 5.1 fusion.384
  1223.7 7.2 dynamic-slice_bitcast_fusion.31
  1233.1 4.0 multiply_reduce_fusion.15
  1237.9 5.1 fusion.384
  (981 shorter events, 643.5 us)
Async XLA Ops:
  6.5 33.3 %copy-start.128 = (s32[2]{0:T(128)S(1)}, s32[2]{0:T(128)}, u32[]{:S(2)}) copy-start(s32[2]{0:T(128)} %constant.290) | copy-start | bytes 28
  6.5 33.4 %copy-start.127 = (s32[2]{0:T(128)S(1)}, s32[2]{0:T(128)}, u32[]{:S(2)}) copy-start(s32[2]{0:T(128)} %constant.293) | copy-start | bytes 28
  6.6 33.5 %copy-start.123 = (f32[2,1,1,4096]{3,2,1,0:T(1,128)S(1)}, f32[2,1,1,4096]{3,2,1,0:T(1,128)}, u32[]{:S(2)}) copy-start(f32[2,1,1,4096]{3,2,1,0:T(1,128)} %param.123) | copy-start | bytes 98308
  6.6 33.5 %copy-start.126 = (f32[1,1,4096]{2,1,0:T(1,128)S(1)}, f32[1,1,4096]{2,1,0:T(1,128)}, u32[]{:S(2)}) copy-start(f32[1,1,4096]{2,1,0:T(1,128)} %param.124) | copy-start | bytes 49156
  31.0 49.3 %all-to-all-start = ((s32[1,16,1024]{2,0,1:T(1,128)}), s32[1,16,1024]{2,0,1:T(1,128)S(1)}, u32[]{:S(2)}, u32[]{:S(2)}) async-start(s32[1,16,1024]{2,0,1:T(1,128)} %bitcast.8), calls=%async_computation | async-start | bytes 131072 | tf_op jit(solution)/shard_map/all_to_all | solution.py:192
  80.2 14.6 %all-to-all-start.1 = ((f32[3,16,1024]{2,0,1:T(4,128)}), f32[3,16,1024]{2,0,1:T(4,128)S(1)}, u32[]{:S(2)}, u32[]{:S(2)}) async-start(f32[3,16,1024]{2,0,1:T(4,128)} %copy.2075), calls=%async_computation.1 | async-start | bytes 524288 | tf_op jit(solution)/shard_map/all_to_all | solution.py:191
  87.5 130.0 %all-gather.3.cloned.1.call-start = ((), (), s32[]{:S(2)}) async-start(), calls=%async_computation.2 | async-start | bytes 2359296 | tf_op jit(solution)/shard_map/all_gather | solution.py:197
  235.6 396.5 %copy-start.9 = (f32[20,16,64]{2,0,1:T(8,128)}, f32[20,16,64]{2,0,1:T(8,128)S(1)}, u32[]{:S(2)}) copy-start(f32[20,16,64]{2,0,1:T(8,128)S(1)} %fusion.27) | copy-start | bytes 245764
  246.5 181.3 %copy-start.42 = (f32[20,4,16]{0,2,1:T(8,128)}, f32[20,4,16]{0,2,1:T(8,128)S(1)}, u32[]{:S(2)}) copy-start(f32[20,4,16]{0,2,1:T(8,128)S(1)} %fusion.30) | copy-start | bytes 15364
  457.5 31.1 %copy-start.117 = (f32[20,20]{1,0:T(8,128)S(1)}, f32[20,20]{1,0:T(8,128)}, u32[]{:S(2)}) copy-start(f32[20,20]{1,0:T(8,128)} %constant.268.clone) | copy-start | bytes 4804
  457.5 32.1 %copy-start.115 = (f32[20,20]{1,0:T(8,128)S(1)}, f32[20,20]{1,0:T(8,128)}, u32[]{:S(2)}) copy-start(f32[20,20]{1,0:T(8,128)} %constant.270.clone) | copy-start | bytes 4804
  457.8 36.9 %copy-start.93 = (f32[20,20,1]{1,0,2:T(8,128)S(1)}, f32[20,20,1]{1,0,2:T(8,128)}, u32[]{:S(2)}) copy-start(f32[20,20,1]{1,0,2:T(8,128)} %constant.308) | copy-start | bytes 4804
  457.9 37.2 %copy-start.90 = (f32[20,20,1]{1,0,2:T(8,128)S(1)}, f32[20,20,1]{1,0,2:T(8,128)}, u32[]{:S(2)}) copy-start(f32[20,20,1]{1,0,2:T(8,128)} %constant.303) | copy-start | bytes 4804
  457.9 37.4 %copy-start.87 = (f32[20,20,1]{1,0,2:T(8,128)S(1)}, f32[20,20,1]{1,0,2:T(8,128)}, u32[]{:S(2)}) copy-start(f32[20,20,1]{1,0,2:T(8,128)} %constant.310) | copy-start | bytes 4804
  457.9 37.7 %copy-start.86 = (f32[20,20,1]{1,0,2:T(8,128)S(1)}, f32[20,20,1]{1,0,2:T(8,128)}, u32[]{:S(2)}) copy-start(f32[20,20,1]{1,0,2:T(8,128)} %constant.309) | copy-start | bytes 4804
  457.9 38.0 %copy-start.36 = (f32[20,540,1]{1,0,2:T(8,128)S(1)}, f32[20,540,1]{1,0,2:T(8,128)}, u32[]{:S(2)}) copy-start(f32[20,540,1]{1,0,2:T(8,128)} %constant.299) | copy-start | bytes 129604
  459.0 37.4 %copy-start.34 = (f32[20,540,1]{1,0,2:T(8,128)S(1)}, f32[20,540,1]{1,0,2:T(8,128)}, u32[]{:S(2)}) copy-start(f32[20,540,1]{1,0,2:T(8,128)} %constant.300) | copy-start | bytes 129604
  459.0 37.9 %copy-start.32 = (f32[20,540,1]{1,0,2:T(8,128)S(1)}, f32[20,540,1]{1,0,2:T(8,128)}, u32[]{:S(2)}) copy-start(f32[20,540,1]{1,0,2:T(8,128)} %constant.301) | copy-start | bytes 129604
  459.0 38.4 %copy-start.31 = (f32[20,540,1]{1,0,2:T(8,128)S(1)}, f32[20,540,1]{1,0,2:T(8,128)}, u32[]{:S(2)}) copy-start(f32[20,540,1]{1,0,2:T(8,128)} %constant.302) | copy-start | bytes 129604
  460.9 35.0 %copy-start.56 = (f32[540,2,32]{0,2,1:T(8,128)S(1)}, f32[540,2,32]{0,2,1:T(8,128)}, u32[]{:S(2)}) copy-start(f32[540,2,32]{0,2,1:T(8,128)} %concatenate.160) | copy-start | bytes 414724
  460.9 36.6 %copy-start.55 = (f32[540,2,32]{0,2,1:T(8,128)S(1)}, f32[540,2,32]{0,2,1:T(8,128)}, u32[]{:S(2)}) copy-start(f32[540,2,32]{0,2,1:T(8,128)} %concatenate.163) | copy-start | bytes 414724
  461.9 36.3 %copy-start.94 = (f32[20,20,1]{1,0,2:T(8,128)S(1)}, f32[20,20,1]{1,0,2:T(8,128)}, u32[]{:S(2)}) copy-start(f32[20,20,1]{1,0,2:T(8,128)} %constant.308) | copy-start | bytes 4804
  567.5 30.5 %collective-permute-start.16 = (f32[20,4,3]{0,2,1:T(4,128)S(1)}, f32[20,4,3]{0,2,1:T(4,128)S(1)}, u32[]{:S(2)}, u32[]{:S(2)}) collective-permute-start(f32[20,4,3]{0,2,1:T(4,128)S(1)} %get-tuple-element.364), channel_id=1, source_target_pairs={{0,8},{8,16},{16,24},{24,32},{32,40},{40,48},{48,56},{56,64},{64,7... | collective-permute-start | bytes 2888 | tf_op jit(solution)/shard_map/ppermute | solution.py:22
  569.5 32.6 %collective-permute-start.17 = (f32[20,4,3]{0,2,1:T(4,128)S(1)}, f32[20,4,3]{0,2,1:T(4,128)S(1)}, u32[]{:S(2)}, u32[]{:S(2)}) collective-permute-start(f32[20,4,3]{0,2,1:T(4,128)S(1)} %get-tuple-element.365), channel_id=1, source_target_pairs={{8,0},{16,8},{24,16},{32,24},{40,32},{48,40},{56,48},{64,56},{72,6... | collective-permute-start | bytes 2888 | tf_op jit(solution)/shard_map/ppermute | solution.py:23
  581.6 24.4 %collective-permute-start.12 = (f32[20,8,3]{2,0,1:T(8,128)S(1)}, f32[20,8,3]{2,0,1:T(8,128)S(1)}, u32[]{:S(2)}, u32[]{:S(2)}) collective-permute-start(f32[20,8,3]{2,0,1:T(8,128)S(1)} %get-tuple-element.360), channel_id=1, source_target_pairs={{0,8},{8,16},{16,24},{24,32},{32,40},{40,48},{48,56},{56,64},{64,7... | collective-permute-start | bytes 5768 | tf_op jit(solution)/shard_map/ppermute | solution.py:22
  583.5 26.5 %collective-permute-start.13 = (f32[20,8,3]{2,0,1:T(8,128)}, f32[20,8,3]{2,0,1:T(8,128)S(1)}, u32[]{:S(2)}, u32[]{:S(2)}) collective-permute-start(f32[20,8,3]{2,0,1:T(8,128)} %get-tuple-element.361), channel_id=1, source_target_pairs={{8,0},{16,8},{24,16},{32,24},{40,32},{48,40},{56,48},{64,56},{72,6... | collective-permute-start | bytes 5768 | tf_op jit(solution)/shard_map/ppermute | solution.py:23
  587.4 36.0 %collective-permute-start.8 = (f32[20,16,3]{2,0,1:T(8,128)}, f32[20,16,3]{2,0,1:T(8,128)S(1)}, u32[]{:S(2)}, u32[]{:S(2)}) collective-permute-start(f32[20,16,3]{2,0,1:T(8,128)} %get-tuple-element.356), channel_id=1, source_target_pairs={{0,8},{8,16},{16,24},{24,32},{32,40},{40,48},{48,56},{56,64},{64,7... | collective-permute-start | bytes 11528 | tf_op jit(solution)/shard_map/ppermute | solution.py:22
  598.1 27.2 %collective-permute-start.9 = (f32[20,16,3]{2,0,1:T(8,128)}, f32[20,16,3]{2,0,1:T(8,128)}, u32[]{:S(2)}, u32[]{:S(2)}) collective-permute-start(f32[20,16,3]{2,0,1:T(8,128)} %get-tuple-element.357), channel_id=1, source_target_pairs={{8,0},{16,8},{24,16},{32,24},{40,32},{48,40},{56,48},{64,56},{72,6... | collective-permute-start | bytes 11528 | tf_op jit(solution)/shard_map/ppermute | solution.py:23
  602.0 30.1 %copy-start.122 = (f32[20,4,3]{0,2,1:T(4,128)}, f32[20,4,3]{0,2,1:T(4,128)S(1)}, u32[]{:S(2)}) copy-start(f32[20,4,3]{0,2,1:T(4,128)S(1)} %collective-permute-done.17) | copy-start | bytes 2884
  602.0 65.5 %collective-permute-start.4 = (f32[20,32,3]{2,1,0:T(8,128)}, f32[20,32,3]{2,1,0:T(8,128)S(1)}, u32[]{:S(2)}, u32[]{:S(2)}) collective-permute-start(f32[20,32,3]{2,1,0:T(8,128)} %get-tuple-element.352), channel_id=1, source_target_pairs={{0,8},{8,16},{16,24},{24,32},{32,40},{40,48},{48,56},{56,64},{64,7... | collective-permute-start | bytes 23048 | tf_op jit(solution)/shard_map/ppermute | solution.py:22
  606.0 34.5 %copy-start.73 = (f32[20,8,3]{2,0,1:T(8,128)}, f32[20,8,3]{2,0,1:T(8,128)S(1)}, u32[]{:S(2)}) copy-start(f32[20,8,3]{2,0,1:T(8,128)S(1)} %collective-permute-done.12) | copy-start | bytes 5764
  606.0 66.0 %collective-permute-start.5 = (f32[20,32,3]{2,1,0:T(8,128)}, f32[20,32,3]{2,1,0:T(8,128)S(1)}, u32[]{:S(2)}, u32[]{:S(2)}) collective-permute-start(f32[20,32,3]{2,1,0:T(8,128)} %get-tuple-element.353), channel_id=1, source_target_pairs={{8,0},{16,8},{24,16},{32,24},{40,32},{48,40},{56,48},{64,56},{72,6... | collective-permute-start | bytes 23048 | tf_op jit(solution)/shard_map/ppermute | solution.py:23
  610.6 133.6 %collective-permute-start = (f32[3,32,32,1]{2,1,3,0:T(8,128)}, f32[3,32,32,1]{2,1,3,0:T(8,128)}, u32[]{:S(2)}, u32[]{:S(2)}) collective-permute-start(f32[3,32,32,1]{2,1,3,0:T(8,128)} %copy.2079), channel_id=1, source_target_pairs={{0,8},{8,16},{16,24},{24,32},{32,40},{40,48},{48,56},{56,64},{64,7... | collective-permute-start | bytes 36872 | tf_op jit(solution)/shard_map/ppermute | solution.py:22
  623.4 24.9 %collective-permute-start.18 = (f32[20,3,22]{0,2,1:T(8,128)}, f32[20,3,22]{0,2,1:T(8,128)}, u32[]{:S(2)}, u32[]{:S(2)}) collective-permute-start(f32[20,3,22]{0,2,1:T(8,128)} %get-tuple-element.362), channel_id=1, source_target_pairs={{0,2},{2,4},{4,6},{1,3},{3,5},{5,7},{8,10},{10,12},{12,14},{9,11},... | collective-permute-start | bytes 15848 | tf_op jit(solution)/shard_map/ppermute | solution.py:22
  625.3 35.8 %copy-start.63 = (f32[20,540]{1,0:T(8,128)S(1)}, f32[20,540]{1,0:T(8,128)}, u32[]{:S(2)}) copy-start(f32[20,540]{1,0:T(8,128)} %constant.263.clone) | copy-start | bytes 129604
  625.3 36.0 %copy-start.61 = (f32[20,540]{1,0:T(8,128)S(1)}, f32[20,540]{1,0:T(8,128)}, u32[]{:S(2)}) copy-start(f32[20,540]{1,0:T(8,128)} %constant.264.clone) | copy-start | bytes 129604
  625.3 27.4 %collective-permute-start.19 = (f32[20,3,22]{0,2,1:T(8,128)}, f32[20,3,22]{0,2,1:T(8,128)}, u32[]{:S(2)}, u32[]{:S(2)}) collective-permute-start(f32[20,3,22]{0,2,1:T(8,128)} %get-tuple-element.363), channel_id=1, source_target_pairs={{2,0},{4,2},{6,4},{3,1},{5,3},{7,5},{10,8},{12,10},{14,12},{11,9},... | collective-permute-start | bytes 15848 | tf_op jit(solution)/shard_map/ppermute | solution.py:23
  633.3 28.4 %copy-start.57 = (f32[20,540]{1,0:T(8,128)S(1)}, f32[20,540]{1,0:T(8,128)}, u32[]{:S(2)}) copy-start(f32[20,540]{1,0:T(8,128)} %constant.266.clone) | copy-start | bytes 129604
  648.2 102.1 %collective-permute-start.1 = (f32[3,32,32,1]{2,1,3,0:T(8,128)}, f32[3,32,32,1]{2,1,3,0:T(8,128)}, u32[]{:S(2)}, u32[]{:S(2)}) collective-permute-start(f32[3,32,32,1]{2,1,3,0:T(8,128)} %copy.2080), channel_id=1, source_target_pairs={{8,0},{16,8},{24,16},{32,24},{40,32},{48,40},{56,48},{64,56},{72,6... | collective-permute-start | bytes 36872 | tf_op jit(solution)/shard_map/ppermute | solution.py:23
  652.8 42.0 %collective-permute-start.14 = (f32[20,3,38]{2,0,1:T(8,128)}, f32[20,3,38]{2,0,1:T(8,128)}, u32[]{:S(2)}, u32[]{:S(2)}) collective-permute-start(f32[20,3,38]{2,0,1:T(8,128)} %get-tuple-element.358), channel_id=1, source_target_pairs={{0,2},{2,4},{4,6},{1,3},{3,5},{5,7},{8,10},{10,12},{12,14},{9,11},... | collective-permute-start | bytes 27368 | tf_op jit(solution)/shard_map/ppermute | solution.py:22
  667.5 31.7 %collective-permute-start.15 = (f32[20,3,38]{2,0,1:T(8,128)}, f32[20,3,38]{2,0,1:T(8,128)S(1)}, u32[]{:S(2)}, u32[]{:S(2)}) collective-permute-start(f32[20,3,38]{2,0,1:T(8,128)} %get-tuple-element.359), channel_id=1, source_target_pairs={{2,0},{4,2},{6,4},{3,1},{5,3},{7,5},{10,8},{12,10},{14,12},{11,9},... | collective-permute-start | bytes 27368 | tf_op jit(solution)/shard_map/ppermute | solution.py:23
  672.8 85.2 %collective-permute-start.10 = (f32[20,3,70]{2,0,1:T(8,128)}, f32[20,3,70]{2,0,1:T(8,128)}, u32[]{:S(2)}, u32[]{:S(2)}) collective-permute-start(f32[20,3,70]{2,0,1:T(8,128)} %get-tuple-element.354), channel_id=1, source_target_pairs={{0,2},{2,4},{4,6},{1,3},{3,5},{5,7},{8,10},{10,12},{12,14},{9,11},... | collective-permute-start | bytes 50408 | tf_op jit(solution)/shard_map/ppermute | solution.py:22
  694.7 67.8 %collective-permute-start.11 = (f32[20,3,70]{2,0,1:T(8,128)}, f32[20,3,70]{2,0,1:T(8,128)}, u32[]{:S(2)}, u32[]{:S(2)}) collective-permute-start(f32[20,3,70]{2,0,1:T(8,128)} %get-tuple-element.355), channel_id=1, source_target_pairs={{2,0},{4,2},{6,4},{3,1},{5,3},{7,5},{10,8},{12,10},{14,12},{11,9},... | collective-permute-start | bytes 50408 | tf_op jit(solution)/shard_map/ppermute | solution.py:23
  699.3 201.4 %collective-permute-start.6 = (f32[20,3,134]{2,1,0:T(4,128)}, f32[20,3,134]{2,1,0:T(4,128)}, u32[]{:S(2)}, u32[]{:S(2)}) collective-permute-start(f32[20,3,134]{2,1,0:T(4,128)} %get-tuple-element.348), channel_id=1, source_target_pairs={{0,2},{2,4},{4,6},{1,3},{3,5},{5,7},{8,10},{10,12},{12,14},{9,11},... | collective-permute-start | bytes 96488 | tf_op jit(solution)/shard_map/ppermute | solution.py:22
  744.2 156.5 %collective-permute-start.7 = (f32[20,3,134]{2,1,0:T(4,128)}, f32[20,3,134]{2,1,0:T(4,128)}, u32[]{:S(2)}, u32[]{:S(2)}) collective-permute-start(f32[20,3,134]{2,1,0:T(4,128)} %get-tuple-element.349), channel_id=1, source_target_pairs={{2,0},{4,2},{6,4},{3,1},{5,3},{7,5},{10,8},{12,10},{14,12},{11,9},... | collective-permute-start | bytes 96488 | tf_op jit(solution)/shard_map/ppermute | solution.py:23
  755.5 377.6 %collective-permute-start.2 = (f32[3,32,1,130]{3,1,2,0:T(8,128)}, f32[3,32,1,130]{3,1,2,0:T(8,128)}, u32[]{:S(2)}, u32[]{:S(2)}) collective-permute-start(f32[3,32,1,130]{3,1,2,0:T(8,128)} %copy.2083), channel_id=1, source_target_pairs={{0,2},{2,4},{4,6},{1,3},{3,5},{5,7},{8,10},{10,12},{12,14},{9,11},... | collective-permute-start | bytes 149768 | tf_op jit(solution)/shard_map/ppermute | solution.py:22
  758.0 376.1 %collective-permute-start.3 = (f32[3,32,1,130]{3,1,2,0:T(8,128)}, f32[3,32,1,130]{3,1,2,0:T(8,128)}, u32[]{:S(2)}, u32[]{:S(2)}) collective-permute-start(f32[3,32,1,130]{3,1,2,0:T(8,128)} %copy.2084), channel_id=1, source_target_pairs={{2,0},{4,2},{6,4},{3,1},{5,3},{7,5},{10,8},{12,10},{14,12},{11,9},... | collective-permute-start | bytes 149768 | tf_op jit(solution)/shard_map/ppermute | solution.py:23
  842.5 28.3 %copy-start.13 = (f32[20,8,32]{0,2,1:T(8,128)S(1)}, f32[20,8,32]{0,2,1:T(8,128)}, u32[]{:S(2)}) copy-start(f32[20,8,32]{0,2,1:T(8,128)} %copy.2175) | copy-start | bytes 61444
  (109 other events, 715.6 us)
Sparse Core Ops, SparseCore 0:
  182.6 10.9 all-gather.2
where the time goes:
time: 1270 us; the launch traced here: 1260 us
  local copies, waits for them, and re-layouts  764 us (60%)
  blocking collectives  177 us (14%)
  matrix products  96.1 us (8%)
  starting transfers between devices  88.1 us (7%)
  other arithmetic  82.5 us (6%)
  loops' own time  23 us (2%)
  between operations  17.9 us (1%)
    slice x305, local copies, waits for them, and re-layouts, grouped_far(): padded[:, first_y:first_y + cells_y:2, first_x:first_x + cells_x:2]  335 us
    all_gather x1, blocking collectives, local(): lax.all_gather(coarse_own[None], ('cell', 'level'), axis=0, tiled=True)  177 us
    dot_general x96, matrix products, apply_matrix(): jnp.einsum('ij,jyx->iyx', jnp.asarray(matrix, dtype=jnp.float32), level_f...  89.4 us
    unnamed x315, local copies, waits for them, and re-layouts  80.3 us
    concatenate x28, local copies, waits for them, and re-layouts, grouped_far(): jnp.concatenate(pieces, axis=0)  77.2 us
    scatter x1, local copies, waits for them, and re-layouts, local(): resident.at[:, arrived_at.reshape(-1)]  62.4 us
    ppermute x10, starting transfers between devices, with_halo(): after = lax.ppermute(first, axis, down)  53.4 us
    reduce_sum x8, other arithmetic, near_band(): real_sum = real_sum + jnp.sum(weight * gap_x, axis=1)  36.7 us
  transfers between devices with their start and end apart: 23, of which 1 were waited for; matrix products, arithmetic and copies ran while one was open for 45% of the time, Pallas kernels for 0%

commit v1 on v0

--- a/solution.py
+++ b/solution.py
@@ -169,6 +169,15 @@
 def local(
     resident_pos, resident_strength, mover_pos, mover_strength, mover_owner, mover_leaf, mover_slot
 ):
+
+    def change_gates(sample):
+        return jnp.concatenate(
+            lax.all_to_all(
+                jnp.stack([sample] * lax.axis_size(("cell", "level"))), ("cell", "level"), 0, 0
+            ),
+            axis=0,
+        )
+
     cell_count = lax.axis_size("cell")
     level_count = lax.axis_size("level")
     half_slots, cells_y, cells_x = resident_strength.shape
@@ -204,7 +213,7 @@
     framed_levels = [framing(owned[k]) for k in range(HALO_LEVELS)]
     coarse_own = owned[HALO_LEVELS]
     channels, coarse_y, coarse_x = coarse_own.shape
-    collected = lax.all_gather(coarse_own[None], ("cell", "level"), axis=0, tiled=True)
+    collected = change_gates(coarse_own[None])
     coarse_grid = collected.reshape(cell_count, level_count, channels, coarse_y, coarse_x)
     coarse_grid = coarse_grid.transpose(2, 1, 3, 0, 4).reshape(
         channels, level_count * coarse_y, cell_count * coarse_x

time: 1270 us -> 1020 us (0.80)
  the two profiles are of different devices: /device:TPU:10 before, /device:TPU:40 now
where the time goes in v1:
time: 1020 us; the launch traced here: 1010 us
  local copies, waits for them, and re-layouts  714 us (70%)
  starting transfers between devices  95.8 us (9%)
  other arithmetic  76 us (7%)
  matrix products  71.5 us (7%)
  loops' own time  24.4 us (2%)
  between operations  18 us (2%)
    slice x305, local copies, waits for them, and re-layouts, grouped_far(): padded[:, first_y:first_y + cells_y:2, first_x:first_x + cells_x:2]  315 us
    unnamed x320, local copies, waits for them, and re-layouts  82 us
    concatenate x28, local copies, waits for them, and re-layouts, grouped_far(): jnp.concatenate(pieces, axis=0)  70.2 us
    dot_general x96, matrix products, apply_matrix(): jnp.einsum('ij,jyx->iyx', jnp.asarray(matrix, dtype=jnp.float32), level_f...  66.8 us
    scatter x1, local copies, waits for them, and re-layouts, local(): resident.at[:, arrived_at.reshape(-1)]  62.4 us
    ppermute x10, starting transfers between devices, with_halo(): after = lax.ppermute(first, axis, down)  48.8 us
    reduce_sum x8, other arithmetic, near_band(): real_sum = real_sum + jnp.sum(weight * gap_x, axis=1)  36.7 us
    slice x1, local copies, waits for them, and re-layouts, local(): far_real, far_imag = evaluate(local_field, particles[0], particles[1])  35 us
  transfers between devices with their start and end apart: 24, of which 1 were waited for; matrix products, arithmetic and copies ran while one was open for 60% of the time, Pallas kernels for 0%

profile of v1, /device:TPU:40, one launch (start us, length us, event | category | flops | bytes accessed | tf_op | source)
XLA Modules:
  0.0 1006.6 jit_solution(7150480751780002980)
XLA Ops:
  7.4 4.6 reduce-window.6
  14.8 16.1 %scatter_custom_fusion.1 = s32[16384]{0:T(1024)} fusion(s32[4096]{0:T(1024)S(1)} %broadcast_select_fusion.1, s32[4096]{0:T(1024)S(1)} %bitcast.978, s32[]{:T(128)} %constant.220.clone.1), kind=kCustom, calls=%fused_computation.410 | custom fusion | bytes 65540
  31.0 7.9 all-to-all-start
  40.4 14.4 %scatter_custom_fusion.2 = f32[3,16384]{0,1:T(8,128)} fusion(s32[4096]{0:T(1024)S(1)} %broadcast_select_fusion, f32[4096,3]{1,0:T(8,128)S(1)} %copy.2070, f32[]{:T(128)} %constant.218.clone.1), kind=kCustom, calls=%fused_computation.103 | custom fusion | bytes 196612
  54.8 5.9 copy.2071
  61.6 16.0 %copy.2072 = f32[3,65536]{0,1:T(8,128)} copy(f32[3,65536]{1,0:T(4,128)S(1)} %pad_maximum_fusion.1) | data formatting | bytes 1572864 | tf_op jit(solution)/shard_map/concatenate | solution.py:203
  77.6 7.2 all-to-all-start.1
  84.9 6.7 all-to-all-done.1
  91.6 5.0 copy.2073
  96.6 62.4 %scatter_fusion = f32[3,65536]{0,1:T(8,128)} fusion(f32[3,65536]{0,1:T(8,128)} %copy.2072, s32[16384]{0:T(1024)S(1)} %bitcast.960, f32[16384,3]{1,0:T(8,128)} %copy.2073), kind=kCustom, calls=%fused_computation | custom fusion | bytes 655360 | tf_op jit(solution)/shard_map/scatter | solution.py:204
  159.0 20.2 %copy.2584 = f32[3,16,32,128]{3,2,1,0:T(8,128)} copy(f32[3,16,32,128]{0,3,2,1:T(8,128)} %bitcast.915) | data formatting | bytes 1572864 | tf_op jit(solution)/shard_map/reshape | solution.py:205
  179.2 35.0 %slice_reduce_fusion.1 = (f32[65536]{0:T(1024)}, f32[65536]{0:T(1024)}) fusion(f32[3,65536]{0,1:T(8,128)} %scatter_fusion), kind=kLoop, calls=%fused_computation.102 | loop fusion | bytes 1048576 | tf_op jit(solution)/shard_map/slice | solution.py:242
  247.7 8.6 all-to-all-start.2
  259.7 4.6 collective-permute-start.17
  266.2 6.0 collective-permute-start.13
  281.7 6.0 collective-permute-start.9
  292.3 6.0 collective-permute-start.5
  332.7 6.0 collective-permute-start.1
  351.7 3.6 collective-permute-start.15
  360.3 3.9 slice.1880
  379.8 4.2 collective-permute-start.11
  424.4 4.5 collective-permute-start.7
  438.1 4.7 collective-permute-start.3
  575.9 3.8 slice.1871
  611.5 4.0 slice.1884
  647.4 3.7 slice.1894
  716.1 9.6 concatenate.134
  725.7 9.6 concatenate.135
  735.2 9.6 concatenate.136
  744.8 10.0 concatenate.137
  754.9 5.7 convolution_bitcast_fusion.7
  760.6 3.8 convolution_bitcast_fusion.6
  764.4 3.8 convolution_bitcast_fusion.5
  768.2 3.8 convolution_bitcast_fusion.4
  775.7 3.8 pad_maximum_fusion
  779.4 100.6 %while.16 = (s32[]{:T(128)}, f32[4,2,16,8,128]{4,3,2,1,0:T(8,128)}, s32[4]{0:T(128)}, f32[3,32,34,130]{3,2,1,0:T(8,128)}, f32[3,16,32,128]{3,2,1,0:T(8,128)}, /*...) while((s32[]{:T(128)}, f32[4,2,16,8,128]{4,3,2,1,0:T(8,128)}, ...), condition=%wide.region_25.26_spmd.clone, body=%wide.region_6.25_spmd.clone.sunk | while | flops 58737680 | bytes 13898660 | solution.py:269
  785.4 6.7 dynamic-slice_bitcast_fusion.31
  794.4 4.0 multiply_reduce_fusion.15
  798.5 5.1 fusion.384
  810.4 7.3 dynamic-slice_bitcast_fusion.31
  820.0 4.0 multiply_reduce_fusion.15
  824.2 5.1 fusion.384
  836.0 6.8 dynamic-slice_bitcast_fusion.31
  845.2 4.0 multiply_reduce_fusion.15
  849.3 5.1 fusion.384
  861.2 6.6 dynamic-slice_bitcast_fusion.31
  870.0 4.0 multiply_reduce_fusion.15
  874.1 5.1 fusion.384
  (980 shorter events, 569.5 us)
Async XLA Ops:
  6.5 32.9 %copy-start.128 = (s32[2]{0:T(128)S(1)}, s32[2]{0:T(128)}, u32[]{:S(2)}) copy-start(s32[2]{0:T(128)} %constant.290) | copy-start | bytes 28
  6.5 33.0 %copy-start.127 = (s32[2]{0:T(128)S(1)}, s32[2]{0:T(128)}, u32[]{:S(2)}) copy-start(s32[2]{0:T(128)} %constant.293) | copy-start | bytes 28
  6.6 33.1 %copy-start.99 = (f32[2,1,1,4096]{3,2,1,0:T(1,128)S(1)}, f32[2,1,1,4096]{3,2,1,0:T(1,128)}, u32[]{:S(2)}) copy-start(f32[2,1,1,4096]{3,2,1,0:T(1,128)} %param.123) | copy-start | bytes 98308
  6.6 33.1 %copy-start.102 = (f32[1,1,4096]{2,1,0:T(1,128)S(1)}, f32[1,1,4096]{2,1,0:T(1,128)}, u32[]{:S(2)}) copy-start(f32[1,1,4096]{2,1,0:T(1,128)} %param.124) | copy-start | bytes 49156
  31.0 46.6 %all-to-all-start = ((s32[1,16,1024]{2,0,1:T(1,128)}), s32[1,16,1024]{2,0,1:T(1,128)S(1)}, u32[]{:S(2)}, u32[]{:S(2)}) async-start(s32[1,16,1024]{2,0,1:T(1,128)} %bitcast.8), calls=%async_computation | async-start | bytes 131072 | tf_op jit(solution)/shard_map/all_to_all | solution.py:201
  77.6 14.0 %all-to-all-start.1 = ((f32[3,16,1024]{2,0,1:T(4,128)}), f32[3,16,1024]{2,0,1:T(4,128)S(1)}, u32[]{:S(2)}, u32[]{:S(2)}) async-start(f32[3,16,1024]{2,0,1:T(4,128)} %copy.2071), calls=%async_computation.1 | async-start | bytes 524288 | tf_op jit(solution)/shard_map/all_to_all | solution.py:200
  84.8 129.4 %all-gather.2.cloned.1.call-start = ((), (), s32[]{:S(2)}) async-start(), calls=%async_computation.3 | async-start | bytes 2359296 | tf_op jit(solution)/shard_map/all_gather | solution.py:206
  217.9 13.4 %copy-start.67 = (f32[20,20,1]{1,0,2:T(8,128)S(1)}, f32[20,20,1]{1,0,2:T(8,128)}, u32[]{:S(2)}) copy-start(f32[20,20,1]{1,0,2:T(8,128)} %constant.305) | copy-start | bytes 4804
  232.4 84.2 %copy-start.9 = (f32[20,16,64]{2,0,1:T(8,128)}, f32[20,16,64]{2,0,1:T(8,128)S(1)}, u32[]{:S(2)}) copy-start(f32[20,16,64]{2,0,1:T(8,128)S(1)} %fusion.27) | copy-start | bytes 245764
  247.7 634.2 %all-to-all-start.2 = ((f32[64,1,320]{2,1,0:T(1,128)}), f32[64,1,320]{2,1,0:T(1,128)}, u32[]{:S(2)}, u32[]{:S(2)}) async-start(f32[64,1,320]{2,1,0:T(1,128)} %reshape.1376), calls=%async_computation.2 | async-start | bytes 196608 | tf_op jit(solution)/shard_map/all_to_all | solution.py:175
  256.3 25.4 %collective-permute-start.16 = (f32[20,4,3]{0,2,1:T(4,128)S(1)}, f32[20,4,3]{0,2,1:T(4,128)S(1)}, u32[]{:S(2)}, u32[]{:S(2)}) collective-permute-start(f32[20,4,3]{0,2,1:T(4,128)S(1)} %get-tuple-element.364), channel_id=1, source_target_pairs={{0,8},{8,16},{16,24},{24,32},{32,40},{40,48},{48,56},{56,64},{64,7... | collective-permute-start | bytes 2888 | tf_op jit(solution)/shard_map/ppermute | solution.py:22
  259.7 28.1 %collective-permute-start.17 = (f32[20,4,3]{0,2,1:T(4,128)S(1)}, f32[20,4,3]{0,2,1:T(4,128)S(1)}, u32[]{:S(2)}, u32[]{:S(2)}) collective-permute-start(f32[20,4,3]{0,2,1:T(4,128)S(1)} %get-tuple-element.365), channel_id=1, source_target_pairs={{8,0},{16,8},{24,16},{32,24},{40,32},{48,40},{56,48},{64,56},{72,6... | collective-permute-start | bytes 2888 | tf_op jit(solution)/shard_map/ppermute | solution.py:23
  264.3 28.0 %collective-permute-start.12 = (f32[20,8,3]{2,0,1:T(8,128)}, f32[20,8,3]{2,0,1:T(8,128)S(1)}, u32[]{:S(2)}, u32[]{:S(2)}) collective-permute-start(f32[20,8,3]{2,0,1:T(8,128)} %get-tuple-element.360), channel_id=1, source_target_pairs={{0,8},{8,16},{16,24},{24,32},{32,40},{40,48},{48,56},{56,64},{64,7... | collective-permute-start | bytes 5768 | tf_op jit(solution)/shard_map/ppermute | solution.py:22
  266.2 32.1 %collective-permute-start.13 = (f32[20,8,3]{2,0,1:T(8,128)}, f32[20,8,3]{2,0,1:T(8,128)S(1)}, u32[]{:S(2)}, u32[]{:S(2)}) collective-permute-start(f32[20,8,3]{2,0,1:T(8,128)} %get-tuple-element.361), channel_id=1, source_target_pairs={{8,0},{16,8},{24,16},{32,24},{40,32},{48,40},{56,48},{64,56},{72,6... | collective-permute-start | bytes 5768 | tf_op jit(solution)/shard_map/ppermute | solution.py:23
  272.2 38.0 %collective-permute-start.8 = (f32[20,16,3]{2,0,1:T(8,128)}, f32[20,16,3]{2,0,1:T(8,128)S(1)}, u32[]{:S(2)}, u32[]{:S(2)}) collective-permute-start(f32[20,16,3]{2,0,1:T(8,128)} %get-tuple-element.356), channel_id=1, source_target_pairs={{0,8},{8,16},{16,24},{24,32},{32,40},{40,48},{48,56},{56,64},{64,7... | collective-permute-start | bytes 11528 | tf_op jit(solution)/shard_map/ppermute | solution.py:22
  281.7 25.4 %copy-start.97 = (f32[20,4,3]{0,2,1:T(4,128)}, f32[20,4,3]{0,2,1:T(4,128)S(1)}, u32[]{:S(2)}) copy-start(f32[20,4,3]{0,2,1:T(4,128)S(1)} %collective-permute-done.16) | copy-start | bytes 2884
  281.7 31.8 %collective-permute-start.9 = (f32[20,16,3]{2,0,1:T(8,128)}, f32[20,16,3]{2,0,1:T(8,128)}, u32[]{:S(2)}, u32[]{:S(2)}) collective-permute-start(f32[20,16,3]{2,0,1:T(8,128)} %get-tuple-element.357), channel_id=1, source_target_pairs={{8,0},{16,8},{24,16},{32,24},{40,32},{48,40},{56,48},{64,56},{72,6... | collective-permute-start | bytes 11528 | tf_op jit(solution)/shard_map/ppermute | solution.py:23
  287.8 19.3 %copy-start.98 = (f32[20,4,3]{0,2,1:T(4,128)}, f32[20,4,3]{0,2,1:T(4,128)S(1)}, u32[]{:S(2)}) copy-start(f32[20,4,3]{0,2,1:T(4,128)S(1)} %collective-permute-done.17) | copy-start | bytes 2884
  287.8 64.0 %collective-permute-start.4 = (f32[20,32,3]{2,1,0:T(8,128)}, f32[20,32,3]{2,1,0:T(8,128)S(1)}, u32[]{:S(2)}, u32[]{:S(2)}) collective-permute-start(f32[20,32,3]{2,1,0:T(8,128)} %get-tuple-element.352), channel_id=1, source_target_pairs={{0,8},{8,16},{16,24},{24,32},{32,40},{40,48},{48,56},{56,64},{64,7... | collective-permute-start | bytes 23048 | tf_op jit(solution)/shard_map/ppermute | solution.py:22
  292.3 21.3 %copy-start.69 = (f32[20,8,3]{2,0,1:T(8,128)}, f32[20,8,3]{2,0,1:T(8,128)S(1)}, u32[]{:S(2)}) copy-start(f32[20,8,3]{2,0,1:T(8,128)S(1)} %collective-permute-done.12) | copy-start | bytes 5764
  292.3 63.1 %collective-permute-start.5 = (f32[20,32,3]{2,1,0:T(8,128)}, f32[20,32,3]{2,1,0:T(8,128)S(1)}, u32[]{:S(2)}, u32[]{:S(2)}) collective-permute-start(f32[20,32,3]{2,1,0:T(8,128)} %get-tuple-element.353), channel_id=1, source_target_pairs={{8,0},{16,8},{24,16},{32,24},{40,32},{48,40},{56,48},{64,56},{72,6... | collective-permute-start | bytes 23048 | tf_op jit(solution)/shard_map/ppermute | solution.py:23
  298.3 26.6 %copy-start.70 = (f32[20,8,3]{2,0,1:T(8,128)}, f32[20,8,3]{2,0,1:T(8,128)S(1)}, u32[]{:S(2)}) copy-start(f32[20,8,3]{2,0,1:T(8,128)S(1)} %collective-permute-done.13) | copy-start | bytes 5764
  298.3 126.1 %collective-permute-start = (f32[3,32,32,1]{2,1,3,0:T(8,128)}, f32[3,32,32,1]{2,1,3,0:T(8,128)}, u32[]{:S(2)}, u32[]{:S(2)}) collective-permute-start(f32[3,32,32,1]{2,1,3,0:T(8,128)} %copy.2075), channel_id=1, source_target_pairs={{0,8},{8,16},{16,24},{24,32},{32,40},{40,48},{48,56},{56,64},{64,7... | collective-permute-start | bytes 36872 | tf_op jit(solution)/shard_map/ppermute | solution.py:22
  310.2 37.9 %copy-start.38 = (f32[20,16,3]{2,0,1:T(8,128)}, f32[20,16,3]{2,0,1:T(8,128)S(1)}, u32[]{:S(2)}) copy-start(f32[20,16,3]{2,0,1:T(8,128)S(1)} %collective-permute-done.8) | copy-start | bytes 11524
  310.2 22.5 %collective-permute-start.18 = (f32[20,3,22]{0,2,1:T(8,128)}, f32[20,3,22]{0,2,1:T(8,128)}, u32[]{:S(2)}, u32[]{:S(2)}) collective-permute-start(f32[20,3,22]{0,2,1:T(8,128)} %get-tuple-element.362), channel_id=1, source_target_pairs={{0,2},{2,4},{4,6},{1,3},{3,5},{5,7},{8,10},{10,12},{12,14},{9,11},... | collective-permute-start | bytes 15848 | tf_op jit(solution)/shard_map/ppermute | solution.py:22
  313.6 25.2 %collective-permute-start.19 = (f32[20,3,22]{0,2,1:T(8,128)}, f32[20,3,22]{0,2,1:T(8,128)}, u32[]{:S(2)}, u32[]{:S(2)}) collective-permute-start(f32[20,3,22]{0,2,1:T(8,128)} %get-tuple-element.363), channel_id=1, source_target_pairs={{2,0},{4,2},{6,4},{3,1},{5,3},{7,5},{10,8},{12,10},{14,12},{11,9},... | collective-permute-start | bytes 15848 | tf_op jit(solution)/shard_map/ppermute | solution.py:23
  317.7 33.0 %copy-start.53 = (f32[20,540]{1,0:T(8,128)S(1)}, f32[20,540]{1,0:T(8,128)}, u32[]{:S(2)}) copy-start(f32[20,540]{1,0:T(8,128)} %constant.265.clone) | copy-start | bytes 129604
  317.8 33.2 %copy-start.51 = (f32[20,540]{1,0:T(8,128)S(1)}, f32[20,540]{1,0:T(8,128)}, u32[]{:S(2)}) copy-start(f32[20,540]{1,0:T(8,128)} %constant.266.clone) | copy-start | bytes 129604
  332.7 97.7 %collective-permute-start.1 = (f32[3,32,32,1]{2,1,3,0:T(8,128)}, f32[3,32,32,1]{2,1,3,0:T(8,128)}, u32[]{:S(2)}, u32[]{:S(2)}) collective-permute-start(f32[3,32,32,1]{2,1,3,0:T(8,128)} %copy.2076), channel_id=1, source_target_pairs={{8,0},{16,8},{24,16},{32,24},{40,32},{48,40},{56,48},{64,56},{72,6... | collective-permute-start | bytes 36872 | tf_op jit(solution)/shard_map/ppermute | solution.py:23
  338.7 41.1 %collective-permute-start.14 = (f32[20,3,38]{2,0,1:T(8,128)}, f32[20,3,38]{2,0,1:T(8,128)}, u32[]{:S(2)}, u32[]{:S(2)}) collective-permute-start(f32[20,3,38]{2,0,1:T(8,128)} %get-tuple-element.358), channel_id=1, source_target_pairs={{0,2},{2,4},{4,6},{1,3},{3,5},{5,7},{8,10},{10,12},{12,14},{9,11},... | collective-permute-start | bytes 27368 | tf_op jit(solution)/shard_map/ppermute | solution.py:22
  351.7 26.0 %copy-start.22 = (f32[20,32,3]{2,1,0:T(8,128)}, f32[20,32,3]{2,1,0:T(8,128)S(1)}, u32[]{:S(2)}) copy-start(f32[20,32,3]{2,1,0:T(8,128)S(1)} %collective-permute-done.4) | copy-start | bytes 23044
  351.7 32.3 %collective-permute-start.15 = (f32[20,3,38]{2,0,1:T(8,128)}, f32[20,3,38]{2,0,1:T(8,128)S(1)}, u32[]{:S(2)}, u32[]{:S(2)}) collective-permute-start(f32[20,3,38]{2,0,1:T(8,128)} %get-tuple-element.359), channel_id=1, source_target_pairs={{2,0},{4,2},{6,4},{3,1},{5,3},{7,5},{10,8},{12,10},{14,12},{11,9},... | collective-permute-start | bytes 27368 | tf_op jit(solution)/shard_map/ppermute | solution.py:23
  356.1 82.0 %collective-permute-start.10 = (f32[20,3,70]{2,0,1:T(8,128)}, f32[20,3,70]{2,0,1:T(8,128)}, u32[]{:S(2)}, u32[]{:S(2)}) collective-permute-start(f32[20,3,70]{2,0,1:T(8,128)} %get-tuple-element.354), channel_id=1, source_target_pairs={{0,2},{2,4},{4,6},{1,3},{3,5},{5,7},{8,10},{10,12},{12,14},{9,11},... | collective-permute-start | bytes 50408 | tf_op jit(solution)/shard_map/ppermute | solution.py:22
  379.8 63.1 %collective-permute-start.11 = (f32[20,3,70]{2,0,1:T(8,128)}, f32[20,3,70]{2,0,1:T(8,128)}, u32[]{:S(2)}, u32[]{:S(2)}) collective-permute-start(f32[20,3,70]{2,0,1:T(8,128)} %get-tuple-element.355), channel_id=1, source_target_pairs={{2,0},{4,2},{6,4},{3,1},{5,3},{7,5},{10,8},{12,10},{14,12},{11,9},... | collective-permute-start | bytes 50408 | tf_op jit(solution)/shard_map/ppermute | solution.py:23
  384.0 190.5 %collective-permute-start.6 = (f32[20,3,134]{2,1,0:T(4,128)}, f32[20,3,134]{2,1,0:T(4,128)}, u32[]{:S(2)}, u32[]{:S(2)}) collective-permute-start(f32[20,3,134]{2,1,0:T(4,128)} %get-tuple-element.348), channel_id=1, source_target_pairs={{0,2},{2,4},{4,6},{1,3},{3,5},{5,7},{8,10},{10,12},{12,14},{9,11},... | collective-permute-start | bytes 96488 | tf_op jit(solution)/shard_map/ppermute | solution.py:22
  396.1 22.9 %copy-start.72 = (f32[20,4,16]{0,2,1:T(8,128)S(1)}, f32[20,4,16]{0,2,1:T(8,128)}, u32[]{:S(2)}) copy-start(f32[20,4,16]{0,2,1:T(8,128)} %copy.2278) | copy-start | bytes 15364
  404.6 14.8 %copy-start.71 = (f32[20,4,16]{0,2,1:T(8,128)S(1)}, f32[20,4,16]{0,2,1:T(8,128)}, u32[]{:S(2)}) copy-start(f32[20,4,16]{0,2,1:T(8,128)} %copy.2305) | copy-start | bytes 15364
  424.4 150.2 %collective-permute-start.7 = (f32[20,3,134]{2,1,0:T(4,128)}, f32[20,3,134]{2,1,0:T(4,128)}, u32[]{:S(2)}, u32[]{:S(2)}) collective-permute-start(f32[20,3,134]{2,1,0:T(4,128)} %get-tuple-element.349), channel_id=1, source_target_pairs={{2,0},{4,2},{6,4},{3,1},{5,3},{7,5},{10,8},{12,10},{14,12},{11,9},... | collective-permute-start | bytes 96488 | tf_op jit(solution)/shard_map/ppermute | solution.py:23
  435.6 338.1 %collective-permute-start.2 = (f32[3,32,1,130]{3,1,2,0:T(8,128)}, f32[3,32,1,130]{3,1,2,0:T(8,128)}, u32[]{:S(2)}, u32[]{:S(2)}) collective-permute-start(f32[3,32,1,130]{3,1,2,0:T(8,128)} %copy.2079), channel_id=1, source_target_pairs={{0,2},{2,4},{4,6},{1,3},{3,5},{5,7},{8,10},{10,12},{12,14},{9,11},... | collective-permute-start | bytes 149768 | tf_op jit(solution)/shard_map/ppermute | solution.py:22
  438.1 336.5 %collective-permute-start.3 = (f32[3,32,1,130]{3,1,2,0:T(8,128)}, f32[3,32,1,130]{3,1,2,0:T(8,128)}, u32[]{:S(2)}, u32[]{:S(2)}) collective-permute-start(f32[3,32,1,130]{3,1,2,0:T(8,128)} %copy.2080), channel_id=1, source_target_pairs={{2,0},{4,2},{6,4},{3,1},{5,3},{7,5},{10,8},{12,10},{14,12},{11,9},... | collective-permute-start | bytes 149768 | tf_op jit(solution)/shard_map/ppermute | solution.py:23
  522.6 28.4 %copy-start.11 = (f32[20,8,32]{0,2,1:T(8,128)S(1)}, f32[20,8,32]{0,2,1:T(8,128)}, u32[]{:S(2)}) copy-start(f32[20,8,32]{0,2,1:T(8,128)} %copy.2169) | copy-start | bytes 61444
  522.6 28.4 %copy-start.12 = (f32[20,8,32]{0,2,1:T(8,128)S(1)}, f32[20,8,32]{0,2,1:T(8,128)}, u32[]{:S(2)}) copy-start(f32[20,8,32]{0,2,1:T(8,128)} %copy.2171) | copy-start | bytes 61444
  909.3 13.4 %copy-start.82 = (f32[20,20,1]{1,0,2:T(8,128)S(1)}, f32[20,20,1]{1,0,2:T(8,128)}, u32[]{:S(2)}) copy-start(f32[20,20,1]{1,0,2:T(8,128)} %constant.310) | copy-start | bytes 4804
  909.3 13.7 %copy-start.81 = (f32[20,20,1]{1,0,2:T(8,128)S(1)}, f32[20,20,1]{1,0,2:T(8,128)}, u32[]{:S(2)}) copy-start(f32[20,20,1]{1,0,2:T(8,128)} %constant.309) | copy-start | bytes 4804
  909.3 13.9 %copy-start.35 = (f32[20,540,1]{1,0,2:T(8,128)S(1)}, f32[20,540,1]{1,0,2:T(8,128)}, u32[]{:S(2)}) copy-start(f32[20,540,1]{1,0,2:T(8,128)} %constant.299) | copy-start | bytes 129604
  909.3 14.4 %copy-start.33 = (f32[20,540,1]{1,0,2:T(8,128)S(1)}, f32[20,540,1]{1,0,2:T(8,128)}, u32[]{:S(2)}) copy-start(f32[20,540,1]{1,0,2:T(8,128)} %constant.300) | copy-start | bytes 129604
  909.6 14.6 %copy-start.31 = (f32[20,540,1]{1,0,2:T(8,128)S(1)}, f32[20,540,1]{1,0,2:T(8,128)}, u32[]{:S(2)}) copy-start(f32[20,540,1]{1,0,2:T(8,128)} %constant.301) | copy-start | bytes 129604
  909.7 15.1 %copy-start.29 = (f32[20,540,1]{1,0,2:T(8,128)S(1)}, f32[20,540,1]{1,0,2:T(8,128)}, u32[]{:S(2)}) copy-start(f32[20,540,1]{1,0,2:T(8,128)} %constant.302) | copy-start | bytes 129604
  (107 other events, 842.6 us)
Sparse Core Ops, SparseCore 0:
  179.4 11.5 all-gather.1
